TPU v7x, 32 devices: a whole 2x2x4 slice. The times are simulated.
32 devices in a mesh: groups: 2 (over x), adapters: 4 (over y, core), tensor: 4 (over z).
Axes of the slice: x: 2, y: 2, z: 4, core: 2. Of those that a mesh axis runs over, the one named last changes fastest.
Arguments:
- hidden: bfloat16 [8192, 8192], P(('groups', 'adapters'), 'tensor'), parts along dimension 0, may hold values from -480 to 480
- input_norm_scale: bfloat16 [8192], P('tensor'), may hold values from 0.25 to 1.75
- key_value_weight: bfloat16 [8192, 2, 1024], P('tensor'), may hold values from -0.09375 to 0.09375
- adapter_down_weight: bfloat16 [64, 8192, 128], P(('groups', 'adapters'), 'tensor'), parts along dimension 0, may hold values from -0.0625 to 0.0625
- adapter_up_weight: bfloat16 [64, 2, 64, 1024], P(('groups', 'adapters')), parts along dimension 0, may hold values from -0.75 to 0.75
- request_adapter_index: int32 [128], P(('groups', 'adapters')), parts along dimension 0, may hold values from 0 to 31, as said below
- request_token_length: int32 [8, 16], P(('groups', 'adapters')), parts along dimension 0, may hold values from 1 to 128, 1024 in all within a row
- adapter_storage_row: int32 [64], P('groups'), parts along dimension 0, may hold values from 0 to 31, as said below
Outputs:
- keys: bfloat16 [8192, 1024], P(('groups', 'adapters'), 'tensor'), parts along dimension 0
- values: bfloat16 [8192, 1024], P(('groups', 'adapters'), 'tensor'), parts along dimension 0
There are 2 independent parts, one for each index of `groups`. A program takes and returns all parts, laid end to end along the dimension named above; an argument that names none is the same for every part. Nothing has to cross between parts.
Inputs may be any that keep to these rules, and one draw needn't show every extreme that they name: `request_adapter_index`: the requests of one device may use adapters stored in many blocks of rows r * 8 to (r + 1) * 8 - 1, but at most 2 distinct adapters of any one block; every device's requests use exactly 2 distinct adapters of some block. A permutation: adapter a is stored at row adapter_storage_row[a] of adapter_down_weight and adapter_up_weight.
All inputs are finite; a program needn't handle non-finite values.
Results may differ from a plain program's by a relative error of at most 0.0049.
Values may be sent and summed in bfloat16 or wider, within the bound.
A program may use at most 128 MiB of HBM per device.

v0:
```python
import math

import jax
import jax.numpy as jnp
from jax import lax
from jax.sharding import PartitionSpec as P

MODEL_WIDTH = 8192
HD = 128
CAP = 2


def rotate_keys(head_keys, positions):
    half_dim = head_keys.shape[-1] // 2
    exponent = jnp.arange(half_dim, dtype=head_keys.dtype) * (2.0 / head_keys.shape[-1])
    frequency = jnp.exp(-exponent * math.log(10000.0))
    angles = positions.astype(head_keys.dtype)[:, None] * frequency[None, :]
    cosine = jnp.cos(angles)[:, None, :]
    sine_part = jnp.sin(angles)[:, None, :]
    first_half = head_keys[..., :half_dim]
    second_half = head_keys[..., half_dim:]
    return jnp.concatenate(
        [
            first_half * cosine - second_half * sine_part,
            second_half * cosine + first_half * sine_part,
        ],
        axis=-1,
    )


def token_positions(lengths, row_count):
    request_ends = jnp.cumsum(lengths)
    offsets = jnp.arange(row_count, dtype=jnp.int32)
    starts = jnp.max(
        jnp.where(request_ends[None, :] <= offsets[:, None], request_ends[None, :], 0), axis=1
    )
    return offsets - starts


def first_slots(adapter_ids, owner_ids):
    row_count = adapter_ids.shape[-1]
    request_index = jnp.arange(row_count, dtype=jnp.int32)
    same_id = adapter_ids[..., :, None] == adapter_ids[..., None, :]
    before = request_index[None, :] < request_index[:, None]
    first_use = jnp.logical_not(jnp.any(jnp.logical_and(same_id, before), axis=-1))
    first_pos = jnp.min(jnp.where(same_id, request_index, row_count), axis=-1)
    same_owner = owner_ids[..., None, :] == owner_ids[..., :, None]
    earlier = request_index[None, :] < first_pos[..., :, None]
    counted = jnp.logical_and(jnp.logical_and(first_use[..., None, :], same_owner), earlier)
    return (jnp.sum(counted.astype(jnp.int32), axis=-1), first_use)


def apply_up(reduced_rank_product, up_block):
    rank_cols = up_block.shape[1]
    key_part = jnp.dot(
        reduced_rank_product[:, :rank_cols],
        up_block[0].astype(jnp.float32),
        precision=lax.Precision.HIGHEST,
    )
    value_part = jnp.dot(
        reduced_rank_product[:, rank_cols:],
        up_block[1].astype(jnp.float32),
        precision=lax.Precision.HIGHEST,
    )
    return jnp.stack([key_part, value_part], axis=0)


def body(
    hidden,
    input_norm_scale,
    key_value_weight,
    adapter_down_weight,
    adapter_up_weight,
    request_adapter_index,
    request_token_length,
    adapter_storage_row,
):
    tok_rows = hidden.shape[0]
    requests = request_adapter_index.shape[0]
    window_rows = 2 * tok_rows // requests
    storage_row_count = adapter_down_weight.shape[0]
    kv_cols = key_value_weight.shape[2]
    owner_count = lax.axis_size("adapters")
    owner_self = lax.axis_index("adapters")
    widened = hidden.astype(jnp.float32)
    squares = lax.psum(jnp.sum(widened * widened, axis=1), "tensor")
    normed = (
        widened
        * lax.rsqrt(squares / MODEL_WIDTH + 1e-05)[:, None]
        * input_norm_scale.astype(jnp.float32)[None, :]
    ).astype(jnp.bfloat16)
    id_table = jnp.arange(adapter_storage_row.shape[0], dtype=jnp.int32)

    def storage_rows(adapter_ids):
        return jnp.sum(
            jnp.where(adapter_ids[..., None] == id_table, adapter_storage_row, 0), axis=-1
        )

    every_id = lax.all_gather(request_adapter_index, "adapters", axis=0, tiled=True).reshape(
        owner_count, requests
    )
    every_row = storage_rows(every_id)
    every_owner = every_row // storage_row_count
    every_slot, every_first = first_slots(every_id, every_owner)
    mine_first = jnp.logical_and(every_first, every_owner == owner_self)
    picked = jnp.logical_and(
        mine_first[:, :, None], every_slot[:, :, None] == jnp.arange(CAP, dtype=jnp.int32)
    )
    outgoing_token_rows = jnp.sum(
        jnp.where(picked, (every_row % storage_row_count)[:, :, None], 0), axis=1
    )
    own_row = storage_rows(request_adapter_index)
    own_owner = own_row // storage_row_count
    own_slot, unused_first = first_slots(request_adapter_index, own_owner)
    source = own_owner * CAP + own_slot
    lengths = request_token_length[0]
    begins = jnp.cumsum(lengths) - lengths
    keep_index = jnp.arange(window_rows, dtype=jnp.int32)
    padded = jnp.concatenate(
        [normed, jnp.zeros((window_rows, normed.shape[1]), jnp.bfloat16)], axis=0
    )
    plain_projection_sum = jnp.einsum(
        "td,dce->cte", normed, key_value_weight, preferred_element_type=jnp.float32
    )
    outgoing_down_weight = jnp.take(adapter_down_weight, outgoing_token_rows, axis=0)

    def lowrank_window(request, got_a):
        request_token_window = lax.dynamic_slice_in_dim(padded, begins[request], window_rows, 0)
        reduced_rank_product = jnp.dot(
            request_token_window, got_a[source[request]], preferred_element_type=jnp.float32
        )
        return jnp.where(
            (keep_index < lengths[request])[:, None],
            reduced_rank_product,
            jnp.zeros_like(reduced_rank_product),
        )

    def add_rows(carried, start_row, adapter_delta, along):
        current = lax.dynamic_slice_in_dim(carried, start_row, window_rows, along)
        return lax.dynamic_update_slice_in_dim(carried, current + adapter_delta, start_row, along)

    outgoing_up_weight = jnp.take(adapter_up_weight, outgoing_token_rows, axis=0)
    got_a, got_b = (
        lax.all_to_all(outgoing_down_weight, "adapters", split_axis=0, concat_axis=0, tiled=True),
        lax.all_to_all(outgoing_up_weight, "adapters", split_axis=0, concat_axis=0, tiled=True),
    )
    got_a = got_a.reshape(-1, got_a.shape[2], got_a.shape[3])
    got_b = got_b.reshape(-1, got_b.shape[2], got_b.shape[3], got_b.shape[4])

    def accumulate_request(request, carried):
        reduced_rank_product = lowrank_window(request, got_a)
        adapter_delta = apply_up(reduced_rank_product, got_b[source[request]])
        return add_rows(carried, begins[request], adapter_delta, 1)

    start_sum = jnp.concatenate(
        [plain_projection_sum, jnp.zeros((2, window_rows, kv_cols), jnp.float32)], axis=1
    )
    to_reduce = lax.fori_loop(0, requests, accumulate_request, start_sum)[:, :tok_rows]
    summed = lax.psum_scatter(to_reduce, "tensor", scatter_dimension=2, tiled=True)
    positions = token_positions(lengths, tok_rows)
    heads_here = summed.shape[2] // HD
    rotated = rotate_keys(summed[0].reshape(tok_rows, heads_here, HD), positions)
    key_out = rotated.reshape(tok_rows, summed.shape[2]).astype(jnp.bfloat16)
    value_out = summed[1].astype(jnp.bfloat16)
    return (key_out, value_out)


def solution(mesh):
    placed = (
        P(("groups", "adapters"), "tensor"),
        P("tensor"),
        P("tensor", None, None),
        P(("groups", "adapters"), "tensor", None),
        P(("groups", "adapters"), None, None, None),
        P(("groups", "adapters")),
        P(("groups", "adapters"), None),
        P("groups"),
    )
    return jax.shard_map(
        body,
        mesh=mesh,
        in_specs=placed,
        out_specs=(P(("groups", "adapters"), "tensor"), P(("groups", "adapters"), "tensor")),
        check_vma=False,
    )
```

profile of v0, /device:TPU:0, one launch (start us, length us, event | category | flops | bytes accessed | tf_op | source)
XLA Modules:
  0.0 547.0 jit_solution(4184621705579438342)
XLA Ops:
  10.1 6.4 %all-reduce.2 = s32[64]{0:T(128)S(1)} all-reduce(s32[64]{0:T(128)S(1)} %dynamic-update-slice), channel_id=1, replica_groups=mesh['groups'=2,'adapters'=4,'tensor'=4] {'adapters'}, use_global_device_ids=true, to_apply=%add.2 | all-reduce | flops 64 | bytes 512
  18.6 2.0 gather_fusion.1
  20.7 3.2 broadcast_select_fusion.1
  23.8 4.5 all-to-all-start.1
  28.3 5.2 gather_fusion
  33.5 3.1 fusion.10
  36.6 12.0 %psum.7 = f32[1024]{0:T(1024)S(1)} all-reduce(f32[1024]{0:T(1024)S(1)} %fusion.10), channel_id=1, replica_groups=mesh['groups'=2,'adapters'=4,'tensor'=4] {'tensor'}, use_global_device_ids=true, to_apply=%region_1.0 | all-reduce | flops 1024 | bytes 8192 | tf_op jit(solution)/shard_map/psum | solution.py:86
  48.6 4.7 broadcast_select_fusion
  54.1 4.8 all-to-all-start
  59.0 5.1 fusion.12
  64.6 5.2 concatenate.11
  69.8 11.5 %fusion.16 = f32[2,1024,1024]{2,1,0:T(8,128)S(1)} fusion(bf16[2048,2,1024]{2,1,0:T(2,128)(2,1)} %param.12, bf16[1024,2048]{1,0:T(8,128)(2,1)S(1)} %copy-done.2), kind=kOutput, calls=%fused_computation.27 | convolution fusion | flops 8589934592 | bytes 20971520 | tf_op jit(solution)/shard_map/td,dce->cte/dot_general | solution.py:122
  81.3 4.6 concatenate.10
  86.5 20.6 %all-to-all-done = bf16[4,2,2048,128]{3,2,1,0:T(8,128)(2,1)} async-done(((bf16[4,2,2048,128]{3,2,1,0:T(8,128)(2,1)}), bf16[4,2,2048,128]{3,2,1,0:T(8,128)(2,1)}, u32[]{:S(2)}, u32[]{:S(2)}) %all-to-all-start) | async-done | bytes 4194336 | tf_op jit(solution)/shard_map/all_to_all | solution.py:144
  107.2 268.1 %while.14 = (s32[]{:T(128)}, f32[2,1152,1024]{2,1,0:T(8,128)}, s32[16]{0:T(128)S(1)}, s32[16]{0:T(128)S(1)}, bf16[1152,2048]{1,0:T(8,128)(2,1)}, /*index=5*/s32[...) while((s32[]{:T(128)}, f32[2,1152,1024]{2,1,0:T(8,128)}, ...), condition=%wide.region_13.14_spmd.clone, body=%wide.region_12.13_spmd.clone.sunk | while | flops 268976256 | bytes 7733777 | solution.py:158
  113.5 1.6 convolution_select_fusion.2
  119.2 4.7 dynamic_update_slice.9
  130.2 1.6 convolution_select_fusion.2
  136.0 4.7 dynamic_update_slice.9
  147.0 1.6 convolution_select_fusion.2
  152.8 4.7 dynamic_update_slice.9
  169.6 4.7 dynamic_update_slice.9
  186.4 4.7 dynamic_update_slice.9
  197.4 1.6 convolution_select_fusion.2
  203.2 4.7 dynamic_update_slice.9
  214.2 1.6 convolution_select_fusion.2
  219.9 4.7 dynamic_update_slice.9
  230.9 1.6 convolution_select_fusion.2
  236.7 4.7 dynamic_update_slice.9
  247.7 1.6 convolution_select_fusion.2
  253.5 4.7 dynamic_update_slice.9
  264.5 1.6 convolution_select_fusion.2
  270.3 4.7 dynamic_update_slice.9
  287.1 4.7 dynamic_update_slice.9
  298.0 1.6 convolution_select_fusion.2
  303.8 4.7 dynamic_update_slice.9
  314.8 1.6 convolution_select_fusion.2
  320.6 4.7 dynamic_update_slice.9
  337.4 4.7 dynamic_update_slice.9
  354.2 4.5 dynamic_update_slice.9
  370.7 4.5 dynamic_update_slice.9
  375.2 8.4 %slice.46 = f32[2,1024,1024]{2,1,0:T(8,128)} slice(f32[2,1152,1024]{2,1,0:T(8,128)} %get-tuple-element.156), slice={[0:2], [0:1024], [0:1024]} | slice | bytes 16777216 | tf_op jit(solution)/shard_map/slice | solution.py:158
  383.7 3.1 multiply_cosine_fusion
  386.8 142.2 %reduce-scatter.2.cloned.1.call-done = f32[2,1024,256]{2,1,0:T(8,128)} async-done(((f32[2,1024,1024]{2,1,0:T(8,128)}), f32[2,1024,256]{2,1,0:T(8,128)}) %reduce-scatter.2.cloned.1.call-update) | async-done | bytes 2097168 | tf_op jit(solution)/shard_map/reduce_scatter | solution.py:159
  529.0 2.3 slice.61
  531.2 1.9 reshape_squeeze.3
  533.1 2.6 subtract_convert_fusion
  538.1 2.1 fusion.21
  (171 shorter events, 123.4 us)
Async XLA Ops:
  7.2 11.5 %copy-start = (bf16[8,2,64,1024]{3,2,1,0:T(8,128)(2,1)S(1)}, bf16[8,2,64,1024]{3,2,1,0:T(8,128)(2,1)}, u32[]{:S(2)}) copy-start(bf16[8,2,64,1024]{3,2,1,0:T(8,128)(2,1)} %param.14) | copy-start | bytes 6291460
  23.8 30.2 %all-to-all-start.1 = ((bf16[4,2,2,64,1024]{4,3,2,1,0:T(8,128)(2,1)}), bf16[4,2,2,64,1024]{4,3,2,1,0:T(8,128)(2,1)}, u32[]{:S(2)}, u32[]{:S(2)}) async-start(bf16[4,2,2,64,1024]{4,3,2,1,0:T(8,128)(2,1)} %broadcast_select_fusion.1), calls=%async_computation.1 | async-start | bytes 4194304 | tf_op jit(solution)/shard_map/all_to_all | solution.py:145
  28.3 5.2 copy-start.3
  54.1 53.1 %all-to-all-start = ((bf16[4,2,2048,128]{3,2,1,0:T(8,128)(2,1)}), bf16[4,2,2048,128]{3,2,1,0:T(8,128)(2,1)}, u32[]{:S(2)}, u32[]{:S(2)}) async-start(bf16[4,2,2048,128]{3,2,1,0:T(8,128)(2,1)} %broadcast_select_fusion), calls=%async_computation | async-start | bytes 8388608 | tf_op jit(solution)/shard_map/all_to_all | solution.py:144
  58.9 5.2 copy-start.6
  58.9 5.4 copy-start.5
  59.0 470.0 %reduce-scatter.2.cloned.1.call-start = ((), (), s32[]{:S(2)}) async-start(), calls=%async_computation.3 | async-start | bytes 10485760 | tf_op jit(solution)/shard_map/reduce_scatter | solution.py:159
  64.6 5.2 copy-start.2
  81.3 4.6 copy-start.4
  531.2 8.9 %copy-start.1 = (bf16[8,2,64,1024]{3,2,1,0:T(8,128)(2,1)S(1)}, bf16[8,2,64,1024]{3,2,1,0:T(8,128)(2,1)}, u32[]{:S(2)}) copy-start(bf16[8,2,64,1024]{3,2,1,0:T(8,128)(2,1)} %param.14) | copy-start | bytes 6291460
Sparse Core Ops, SparseCore 0:
  383.7 145.1 reduce-scatter.1
where the time goes:
time: 552 us; the launch traced here: 547 us
  waiting for transfers between devices  164 us (30%)
  local copies, waits for them, and re-layouts  138 us (25%)
  matrix products  79.3 us (14%)
  loops' own time  62.8 us (11%)
  other arithmetic  60.5 us (11%)
  blocking collectives  18.4 us (3%)
  between operations  14.9 us (3%)
  starting transfers between devices  9.35 us (2%)
    reduce_scatter x1, waiting for transfers between devices, body(): lax.psum_scatter(to_reduce, 'tensor', scatter_dimension=2, tiled=True)  142 us
    dynamic_update_slice x16, local copies, waits for them, and re-layouts, add_rows(): lax.dynamic_update_slice_in_dim(carried, current + adapter_delta, start_r...  74.7 us
    another operation x1, loops' own time, body(): lax.fori_loop(0, requests, accumulate_request, start_sum)[:, :tok_rows]  62.8 us
    dot_general x16, matrix products, lowrank_window(): jnp.dot(request_token_window, got_a[source[request]], preferred_element_t...  25.3 us
    add x16, other arithmetic, add_rows(): current + adapter_delta  24.2 us
    dot_general x16, matrix products, apply_up(): jnp.dot(reduced_rank_product[:, rank_cols:], up_block[1].astype(jnp.float...  21.3 us
    dot_general x16, matrix products, apply_up(): jnp.dot(reduced_rank_product[:, :rank_cols], up_block[0].astype(jnp.float...  21.2 us
    all_to_all x1, waiting for transfers between devices, body(): lax.all_to_all(outgoing_down_weight, 'adapters', split_axis=0, concat_axi...  20.6 us
  transfers between devices with their start and end apart: 3, of which 3 were waited for; matrix products, arithmetic and copies ran while one was open for 8% of the time, Pallas kernels for 0%

commit v1 on v0

v1 whole, which is shorter than its diff:
```python
import functools
import math

import jax
import jax.numpy as jnp
from jax import lax
from jax.experimental import pallas as pl
from jax.experimental.pallas import tpu as pltpu
from jax.sharding import PartitionSpec as P

MODEL_WIDTH = 8192
HD = 128
CAP = 2
BLOCKS = 4
MESH = pl.DeviceIdType.MESH
F32 = jnp.float32
BF16 = jnp.bfloat16


def kernel(
    owners,
    ranks,
    rows_ref,
    tok_ref,
    freq_ref,
    scale_ref,
    h_hbm,
    w_hbm,
    a_hbm,
    b_hbm,
    key_ref,
    value_ref,
    hs,
    wv,
    av,
    bv,
    out_a,
    got_a,
    out_b,
    got_b,
    part,
    send,
    got_up,
    got_dn,
    low,
    low_send,
    low_got,
    ss,
    load_sem,
    w_sem,
    a_send_sem,
    a_sem,
    b_send_sem,
    b_sem,
    send_sem,
    up_sem,
    dn_sem,
    low_send_sem,
    low_sem,
    ss_send_sem,
    ss_sem,
):
    me = lax.axis_index("adapters")
    t = lax.axis_index("tensor")
    tokens, feats = hs.shape
    tb = tokens // BLOCKS
    cols = key_ref.shape[1]
    rank = bv.shape[2]
    last = ranks - 1
    is_lo = t == 0
    is_hi = t == last
    lower = t < ranks // 2

    def target(k):
        below = jnp.where(k < last - t, last - k, k - (last - t))
        above = jnp.where(k < t, k, last - (k - t))
        return jnp.where(k == last, t, jnp.where(lower, below, above))

    def rows(b):
        return pl.ds(pl.multiple_of(b * tb, tb), tb)

    h_copy = [
        pltpu.make_async_copy(h_hbm.at[rows(b)], hs.at[rows(b)], load_sem.at[2 + b])
        for b in range(BLOCKS)
    ]

    def w_copy(k):
        j = target(k)
        return pltpu.make_async_copy(
            w_hbm.at[:, :, pl.ds(pl.multiple_of(j * cols, 128), cols)], wv.at[j], w_sem.at[k]
        )

    a_copy = pltpu.make_async_copy(a_hbm, av, load_sem.at[0])
    b_copy = pltpu.make_async_copy(
        b_hbm.at[:, :, :, pl.ds(pl.multiple_of(t * cols, 128), cols)], bv, load_sem.at[1]
    )
    for b in range(BLOCKS):
        h_copy[b].start()
    w_copy(0).start()
    a_copy.start()
    b_copy.start()
    for k in range(1, ranks):
        w_copy(k).start()

    ss[...] = jnp.zeros_like(ss)
    got_b[...] = jnp.zeros_like(got_b)

    barrier = pltpu.get_barrier_semaphore()
    for k in range(1, owners):
        pl.semaphore_signal(
            barrier, inc=1, device_id={"adapters": lax.rem(me + k, owners)}, device_id_type=MESH
        )
    for k in range(1, ranks):
        pl.semaphore_signal(
            barrier, inc=1, device_id={"tensor": lax.rem(t + k, ranks)}, device_id_type=MESH
        )
    pl.semaphore_wait(barrier, owners - 1 + ranks - 1)

    def up_copy(j, b):
        return pltpu.make_async_remote_copy(
            src_ref=send.at[j, rows(b)],
            dst_ref=got_up.at[j, rows(b)],
            send_sem=send_sem.at[j, b],
            recv_sem=up_sem.at[j, b],
            device_id={"tensor": lax.rem(t + 1, ranks)},
            device_id_type=MESH,
        )

    def dn_copy(j, b):
        return pltpu.make_async_remote_copy(
            src_ref=send.at[j, rows(b)],
            dst_ref=got_dn.at[j, rows(b)],
            send_sem=send_sem.at[j, b],
            recv_sem=dn_sem.at[j, b],
            device_id={"tensor": lax.rem(t + last, ranks)},
            device_id_type=MESH,
        )

    def low_copy(way, b):
        return pltpu.make_async_remote_copy(
            src_ref=low_send.at[way, rows(b)],
            dst_ref=low_got.at[way, rows(b)],
            send_sem=low_send_sem.at[way, b],
            recv_sem=low_sem.at[way, b],
            device_id={"tensor": lax.rem(t + (1 if way == 0 else last), ranks)},
            device_id_type=MESH,
        )

    def ss_copy(k):
        return pltpu.make_async_remote_copy(
            src_ref=ss.at[t],
            dst_ref=ss.at[t],
            send_sem=ss_send_sem.at[k],
            recv_sem=ss_sem.at[t],
            device_id={"tensor": lax.rem(t + k, ranks)},
            device_id_type=MESH,
        )

    def ss_arrival(k):
        source = lax.rem(t + k, ranks)
        return pltpu.make_async_remote_copy(
            src_ref=ss.at[source],
            dst_ref=ss.at[source],
            send_sem=ss_send_sem.at[k],
            recv_sem=ss_sem.at[source],
            device_id={"tensor": source},
            device_id_type=MESH,
        )

    def a_move(k, source, s):
        d = lax.rem(me + k, owners)
        return pltpu.make_async_remote_copy(
            src_ref=out_a.at[k - 1, s],
            dst_ref=got_a.at[source * CAP + s],
            send_sem=a_send_sem.at[k, s],
            recv_sem=a_sem.at[source, s],
            device_id={"adapters": d},
            device_id_type=MESH,
        )

    def b_move(k, source, s, c):
        d = lax.rem(me + k, owners)
        return pltpu.make_async_remote_copy(
            src_ref=out_b.at[k - 1, s, c],
            dst_ref=got_b.at[
                source * CAP + s, pl.ds(c * rank, rank), pl.ds(c * cols, cols)
            ],
            send_sem=b_send_sem.at[k, s, c],
            recv_sem=b_sem.at[source, s, c],
            device_id={"adapters": d},
            device_id_type=MESH,
        )

    ones = jnp.ones((8, feats), BF16)
    contract = (((1,), (1,)), ((), ()))
    for b in range(BLOCKS):
        h_copy[b].wait()
    step = 128

    def prepare(i, carry):
        sl = pl.ds(pl.multiple_of(i * step, step), step)
        h = hs[sl, :].astype(F32)
        sq = h * h
        hi = sq.astype(BF16)
        lo = (sq - hi.astype(F32)).astype(BF16)
        total = lax.dot_general(ones, hi, contract, preferred_element_type=F32)
        total += lax.dot_general(ones, lo, contract, preferred_element_type=F32)
        ss[t, :, sl] = total
        hs[sl, :] = (h * scale_ref[...]).astype(BF16)
        return carry

    lax.fori_loop(0, tokens // step, prepare, 0)
    for k in range(1, ranks):
        ss_copy(k).start()

    def project(k):
        j = target(k)
        w_copy(k).wait()

        def one(b, carry):
            x = hs[rows(b), :]
            for c in range(2):
                y = jnp.dot(x, wv[j, c], preferred_element_type=F32)
                part[j, rows(b), pl.ds(c * cols, cols)] = y
                if k < last:

                    @pl.when(is_lo | is_hi)
                    def _():
                        send[j, rows(b), pl.ds(c * cols, cols)] = y.astype(BF16)

            if k < last:

                @pl.when(is_lo)
                def _():
                    up_copy(j, b).start()

                @pl.when(is_hi)
                def _():
                    dn_copy(j, b).start()

            return carry

        lax.fori_loop(0, BLOCKS, one, 0)

    project(0)

    a_copy.wait()
    b_copy.wait()
    piece = min(256, feats)
    order = sorted(range(1, owners), key=lambda k: abs(k - owners // 2))
    for k in order:
        d = lax.rem(me + k, owners)
        for s in range(CAP):
            row = rows_ref[d, s]

            def stage(i, carry):
                sl = pl.ds(pl.multiple_of(i * piece, piece), piece)
                out_a[k - 1, s, sl, :] = av[row, sl, :]
                return carry

            lax.fori_loop(0, feats // piece, stage, 0)
            a_move(k, me, s).start()
    for k in order:
        d = lax.rem(me + k, owners)
        for s in range(CAP):
            row = rows_ref[d, s]
            for c in range(2):
                out_b[k - 1, s, c] = bv[row, c]
                b_move(k, me, s, c).start()
    for s in range(CAP):
        row = rows_ref[me, s]

        def keep(i, carry):
            sl = pl.ds(pl.multiple_of(i * piece, piece), piece)
            got_a[me * CAP + s, sl, :] = av[row, sl, :]
            return carry

        lax.fori_loop(0, feats // piece, keep, 0)
        for c in range(2):
            got_b[me * CAP + s, pl.ds(c * rank, rank), pl.ds(c * cols, cols)] = bv[row, c]

    for k in range(1, ranks):
        project(k)

    def lowrank(slot, first):
        def one(b, carry):
            y = jnp.dot(hs[rows(b), :], got_a[slot], preferred_element_type=F32)
            y = jnp.where(tok_ref[rows(b), 0:1] == slot, y, 0.0)
            if first:
                low[rows(b), :] = y
            else:
                low[rows(b), :] = low[rows(b), :] + y
            return carry

        lax.fori_loop(0, BLOCKS, one, 0)

    for s in range(CAP):
        lowrank(me * CAP + s, s == 0)

    def forward(k):
        ju = last - k
        jd = k

        def one(b, carry):
            @pl.when((t > 0) & (ju > t))
            def _():
                up_copy(ju, b).wait_recv()

                @pl.when(t < last)
                def _():
                    send[ju, rows(b), :] = (
                        part[ju, rows(b), :] + got_up[ju, rows(b), :].astype(F32)
                    ).astype(BF16)
                    up_copy(ju, b).start()

            @pl.when((t < last) & (jd < t))
            def _():
                dn_copy(jd, b).wait_recv()

                @pl.when(t > 0)
                def _():
                    send[jd, rows(b), :] = (
                        part[jd, rows(b), :] + got_dn[jd, rows(b), :].astype(F32)
                    ).astype(BF16)
                    dn_copy(jd, b).start()

            return carry

        lax.fori_loop(0, BLOCKS, one, 0)

    for k in range(last):
        forward(k)

    arrivals = sorted(range(1, owners), key=lambda k: abs(k - owners // 2), reverse=True)
    for k in arrivals:
        source = lax.rem(me + owners - k, owners)
        for s in range(CAP):
            a_move(k, source, s).wait_recv()
            lowrank(source * CAP + s, False)

    def low_start(b, carry):
        mine = low[rows(b), :]

        @pl.when(t == 0)
        def _():
            low_send[0, rows(b), :] = mine.astype(BF16)
            low_copy(0, b).start()

        @pl.when(t == last)
        def _():
            low_send[1, rows(b), :] = mine.astype(BF16)
            low_copy(1, b).start()

        return carry

    lax.fori_loop(0, BLOCKS, low_start, 0)

    for b in range(BLOCKS):

        @pl.when(t > 0)
        def _():
            low_copy(0, b).wait_recv()

            @pl.when(t < last)
            def _():
                low_send[0, rows(b), :] = (
                    low[rows(b), :] + low_got[0, rows(b), :].astype(F32)
                ).astype(BF16)
                low_copy(0, b).start()

        @pl.when(t < last)
        def _():
            low_copy(1, b).wait_recv()

            @pl.when(t > 0)
            def _():
                low_send[1, rows(b), :] = (
                    low[rows(b), :] + low_got[1, rows(b), :].astype(F32)
                ).astype(BF16)
                low_copy(1, b).start()

    for k in range(1, ranks):
        ss_arrival(k).wait_recv()
    for k in arrivals:
        source = lax.rem(me + owners - k, owners)
        for s in range(CAP):
            for c in range(2):
                b_move(k, source, s, c).wait_recv()

    slots = owners * CAP

    def finish(b, carry):
        sl = rows(b)
        total = part[t, sl, :]
        lows = low[sl, :]

        gains = jnp.sum(ss[:, :, sl], axis=0).T[:, 0:1]
        gains = lax.rsqrt(gains * (1.0 / MODEL_WIDTH) + 1e-05)
        part[t, sl, :] = total

        @pl.when(t > 0)
        def _():
            up_copy(t, b).wait_recv()
            part[t, sl, :] = part[t, sl, :] + got_up[t, sl, :].astype(F32)
            low[sl, :] = low[sl, :] + low_got[0, sl, :].astype(F32)

        @pl.when(t < last)
        def _():
            dn_copy(t, b).wait_recv()
            part[t, sl, :] = part[t, sl, :] + got_dn[t, sl, :].astype(F32)
            low[sl, :] = low[sl, :] + low_got[1, sl, :].astype(F32)

        lows = low[sl, :]
        hi = lows.astype(BF16).astype(F32)
        lo = lows - hi
        mine = tok_ref[sl, 0:1]
        picked_hi = jnp.concatenate(
            [jnp.where(mine == s, hi, 0.0).astype(BF16) for s in range(slots)], axis=1
        )
        picked_lo = jnp.concatenate(
            [jnp.where(mine == s, lo, 0.0).astype(BF16) for s in range(slots)], axis=1
        )
        maps = got_b[...].reshape(slots * 2 * rank, 2 * cols)
        total = part[t, sl, :]
        total += jnp.dot(picked_hi, maps, preferred_element_type=F32)
        total += jnp.dot(picked_lo, maps, preferred_element_type=F32)
        total = total * gains
        value_ref[sl, :] = total[:, cols:].astype(BF16)
        angles = tok_ref[sl, 1:2].astype(F32) * freq_ref[...]
        cosine = jnp.cos(angles)
        sine = jnp.sin(angles)
        lane = lax.broadcasted_iota(jnp.int32, sine.shape, 1)
        sine = jnp.where(lane < HD // 2, -sine, sine)
        for head in range(cols // HD):
            x = total[:, head * HD : (head + 1) * HD]
            key_ref[sl, pl.ds(head * HD, HD)] = (
                x * cosine + pltpu.roll(x, HD // 2, 1) * sine
            ).astype(BF16)
        return carry

    lax.fori_loop(0, BLOCKS, finish, 0)

    for k in range(1, ranks):
        ss_copy(k).wait_send()
    for k in range(1, owners):
        for s in range(CAP):
            a_move(k, me, s).wait_send()
            for c in range(2):
                b_move(k, me, s, c).wait_send()

    def drain(b, carry):
        for j in range(ranks):

            @pl.when(j != t)
            def _():
                up_copy(j, b).wait_send()

        @pl.when(t < last)
        def _():
            low_copy(0, b).wait_send()

        @pl.when(t > 0)
        def _():
            low_copy(1, b).wait_send()

        return carry

    lax.fori_loop(0, BLOCKS, drain, 0)


def body(
    hidden,
    input_norm_scale,
    key_value_weight,
    adapter_down_weight,
    adapter_up_weight,
    request_adapter_index,
    request_token_length,
    adapter_storage_row,
):
    tokens, feats = hidden.shape
    requests = request_adapter_index.shape[0]
    stored = adapter_down_weight.shape[0]
    width = key_value_weight.shape[2]
    rank = adapter_up_weight.shape[2]
    owners = lax.axis_size("adapters")
    ranks = lax.axis_size("tensor")
    me = lax.axis_index("adapters")
    cols = width // ranks
    slots = owners * CAP

    id_table = jnp.arange(adapter_storage_row.shape[0], dtype=jnp.int32)

    def storage_rows(ids):
        return jnp.sum(jnp.where(ids[..., None] == id_table, adapter_storage_row, 0), axis=-1)

    every_row = storage_rows(
        lax.all_gather(request_adapter_index, "adapters", axis=0, tiled=True).reshape(
            owners, requests
        )
    )
    held_here = every_row // stored == me
    local = every_row % stored
    least = jnp.min(jnp.where(held_here, local, stored - 1), axis=1)
    most = jnp.max(jnp.where(held_here, local, 0), axis=1)
    wanted = jnp.stack([least, most], axis=1)

    own_row = storage_rows(request_adapter_index)
    own_owner = own_row // stored
    same = own_owner[:, None] == own_owner[None, :]
    own_least = jnp.min(jnp.where(same, own_row[None, :], slots * stored), axis=1)
    own_slot = own_owner * CAP + (own_row != own_least).astype(jnp.int32)
    lengths = request_token_length[0]
    ends = jnp.sum(
        jnp.where(jnp.arange(requests)[None, :] <= jnp.arange(requests)[:, None], lengths, 0),
        axis=1,
    )
    begins = ends - lengths
    offsets = jnp.arange(tokens, dtype=jnp.int32)[:, None]
    inside = (begins <= offsets) & (offsets < ends)
    token_slot = jnp.sum(jnp.where(inside, own_slot, 0), axis=1)
    token_position = jnp.sum(jnp.where(inside, offsets - begins, 0), axis=1)
    token_info = jnp.stack([token_slot, token_position], axis=1)
    half = HD // 2
    exponent = (jnp.arange(HD, dtype=jnp.int32) % half).astype(F32) * (2.0 / HD)
    frequency = jnp.exp(-exponent * math.log(10000.0))[None, :]
    scale = input_norm_scale.astype(F32)[None, :]
    weight = jnp.transpose(key_value_weight, (1, 0, 2))

    vmem = pl.BlockSpec(memory_space=pltpu.VMEM)
    smem = pl.BlockSpec(memory_space=pltpu.SMEM)
    anywhere = pl.BlockSpec(memory_space=pl.ANY)
    dma = pltpu.SemaphoreType.DMA
    return pl.pallas_call(
        functools.partial(kernel, owners, ranks),
        out_shape=(
            jax.ShapeDtypeStruct((tokens, cols), BF16),
            jax.ShapeDtypeStruct((tokens, cols), BF16),
        ),
        in_specs=[smem, vmem, vmem, vmem] + [anywhere] * 4,
        out_specs=(vmem, vmem),
        scratch_shapes=[
            pltpu.VMEM((tokens, feats), BF16),
            pltpu.VMEM((ranks, 2, feats, cols), BF16),
            pltpu.VMEM((stored, feats, 2 * rank), BF16),
            pltpu.VMEM((stored, 2, rank, cols), BF16),
            pltpu.VMEM((owners - 1, CAP, feats, 2 * rank), BF16),
            pltpu.VMEM((slots, feats, 2 * rank), BF16),
            pltpu.VMEM((owners - 1, CAP, 2, rank, cols), BF16),
            pltpu.VMEM((slots, 2 * rank, 2 * cols), BF16),
            pltpu.VMEM((ranks, tokens, 2 * cols), F32),
            pltpu.VMEM((ranks, tokens, 2 * cols), BF16),
            pltpu.VMEM((ranks, tokens, 2 * cols), BF16),
            pltpu.VMEM((ranks, tokens, 2 * cols), BF16),
            pltpu.VMEM((tokens, 2 * rank), F32),
            pltpu.VMEM((2, tokens, 2 * rank), BF16),
            pltpu.VMEM((2, tokens, 2 * rank), BF16),
            pltpu.VMEM((ranks, 8, tokens), F32),
            dma((2 + BLOCKS,)),
            dma((ranks,)),
            dma((owners, CAP)),
            dma((owners, CAP)),
            dma((owners, CAP, 2)),
            dma((owners, CAP, 2)),
            dma((ranks, BLOCKS)),
            dma((ranks, BLOCKS)),
            dma((ranks, BLOCKS)),
            dma((2, BLOCKS)),
            dma((2, BLOCKS)),
            dma((ranks,)),
            dma((ranks,)),
        ],
        compiler_params=pltpu.CompilerParams(
            collective_id=0, has_side_effects=True, vmem_limit_bytes=60 * 1024 * 1024
        ),
        cost_estimate=pl.CostEstimate(
            flops=2 * tokens * feats * (2 * width + slots * 2 * rank),
            bytes_accessed=20 * 1024 * 1024,
            transcendentals=0,
        ),
    )(
        wanted,
        token_info,
        frequency,
        scale,
        hidden,
        weight,
        adapter_down_weight,
        adapter_up_weight,
    )


def solution(mesh):
    placed = (
        P(("groups", "adapters"), "tensor"),
        P("tensor"),
        P("tensor", None, None),
        P(("groups", "adapters"), "tensor", None),
        P(("groups", "adapters"), None, None, None),
        P(("groups", "adapters")),
        P(("groups", "adapters"), None),
        P("groups"),
    )
    return jax.shard_map(
        body,
        mesh=mesh,
        in_specs=placed,
        out_specs=(P(("groups", "adapters"), "tensor"), P(("groups", "adapters"), "tensor")),
        check_vma=False,
    )
```

time: 552 us -> 163 us (0.30)
  waiting for transfers between devices: 164 us -> 0 us
  Pallas kernels: 0 us -> 132 us
  local copies, waits for them, and re-layouts: 138 us -> 16.4 us
  matrix products: 79.3 us -> 0 us
  loops' own time: 62.8 us -> 0 us
  other arithmetic: 60.5 us -> 6.2 us
  between operations: 14.9 us -> 1.33 us
  blocking collectives: 18.4 us -> 6.38 us
  starting transfers between devices: 9.35 us -> 0 us
    reduce_scatter x1 -> x0, waiting for transfers between devices: 142 us -> none  [body(): lax.psum_scatter(to_reduce, 'tensor', scatter_dimension=2, tiled=True)]
    pallas_call x0 -> x1, Pallas kernels: none -> 132 us  [body(): pl.pallas_call(functools.partial(kernel, owners, ranks), out_shape=(jax.S...]
    dot_general x49 -> x0, matrix products: 79.3 us -> none  [the longest x16 25.3 us: lowrank_window(): jnp.dot(request_token_window, got_a[source[request]], preferred_element_t...]
    dynamic_update_slice x16 -> x0, local copies, waits for them, and re-layouts: 74.7 us -> none  [add_rows(): lax.dynamic_update_slice_in_dim(carried, current + adapter_delta, start_r...]
    another operation x1 -> x0, loops' own time: 62.8 us -> none  [body(): lax.fori_loop(0, requests, accumulate_request, start_sum)[:, :tok_rows]]
    dynamic_slice x48 -> x0, local copies, waits for them, and re-layouts: 28.2 us -> none  [the longest x16 9.42 us: lowrank_window(): source[request]]
    add x17 -> x1, other arithmetic: 24.2 us -> 0.01 us  [body(): own_slot = own_owner * CAP + (own_row != own_least).astype(jnp.int32)]
    all_to_all x2 -> x0, waiting for transfers between devices: 21.4 us -> none  [the longest x1 20.6 us: body(): lax.all_to_all(outgoing_down_weight, 'adapters', split_axis=0, concat_axi...]
  transfers between devices with their start and end apart: 3 -> 0, of which waited for: 3 -> 0; matrix products, arithmetic and copies ran while one was open for 8% -> 0% of each run, Pallas kernels for 0% -> 0%
where the time goes in v1:
time: 163 us
  Pallas kernels  132 us (81%)
  local copies, waits for them, and re-layouts  16.4 us (10%)
  blocking collectives  6.38 us (4%)
  other arithmetic  6.2 us (4%)
    pallas_call x1, Pallas kernels, body(): pl.pallas_call(functools.partial(kernel, owners, ranks), out_shape=(jax.S...  132 us
    unnamed x6, local copies, waits for them, and re-layouts  15.1 us
    unnamed x1, blocking collectives  6.38 us

profile of v1, /device:TPU:0, one launch (start us, length us, event | category | flops | bytes accessed | tf_op | source)
XLA Modules:
  0.0 162.5 jit_solution(16669876099873069011)
XLA Ops:
  0.6 1.2 dynamic-slice
  2.5 0.9 select_reduce_fusion.4
  3.4 0.8 select_reduce_fusion.5
  4.2 0.7 fusion.9
  4.8 0.2 select_reduce_fusion.3
  5.0 0.9 dynamic-update-slice
  5.9 6.4 %all-reduce = s32[64]{0:T(128)S(1)} all-reduce(s32[64]{0:T(128)S(1)} %dynamic-update-slice), channel_id=1, replica_groups=mesh['groups'=2,'adapters'=4,'tensor'=4] {'adapters'}, use_global_device_ids=true, to_apply=%add | all-reduce | flops 64 | bytes 512
  12.3 0.6 fusion.8.freq_ref
  12.9 0.1 eq.51
  13.0 0.9 select_reduce_fusion.2
  13.8 0.2 select_reduce_fusion.7
  14.0 0.1 copy.23
  14.1 0.1 copy.22
  14.2 0.7 pad_add_fusion.1.rows_ref
  14.9 0.1 select_reduce_fusion.1
  15.0 1.3 broadcast_in_dim.79
  16.3 1.0 copy.25.tok_ref
  17.3 9.3 %copy.27 = bf16[2048,2,1024]{2,0,1:T(8,128)(2,1)} copy(bf16[2048,2,1024]{2,1,0:T(2,128)(2,1)} %param.10) | data formatting | bytes 16777216 | tf_op args[2]
  26.6 132.2 %shard_map.95 = (bf16[1024,256]{1,0:T(8,128)(2,1)}, bf16[1024,256]{1,0:T(8,128)(2,1)}) custom-call(s32[4,2]{1,0:T(4,128)} %pad_add_fusion.1.rows_ref, s32[1024,2]{1,0:T(8,128)} %copy.25.tok_ref, f32[1,128]{1,0:T(1,128)} %fusion.8.freq_ref, f32[1,2048]{1,0:T(1,128)} %bitcast.19, bf16[1024,2048]{1,0:T(8,128)(2,1)} %h_hbm.1, bf16[2,2048,1024]{2,1,0:T(8,128)(2,1)} %bitcast.16, ...), custom_call_target="tpu_custom_call" | custom-call | flops 12884901888 | bytes 20971520 | tf_op jit(solution)/shard_map/pallas_call | solution.py:534
  158.8 1.9 %copy.31 = bf16[1024,256]{1,0:T(8,128)(2,1)} copy(bf16[1024,256]{1,0:T(8,128)(2,1)} %get-tuple-element.8) | data formatting | bytes 1048576
  160.6 1.9 %copy.32 = bf16[1024,256]{1,0:T(8,128)(2,1)} copy(bf16[1024,256]{1,0:T(8,128)(2,1)} %get-tuple-element.9) | data formatting | bytes 1048576
  (4 shorter events, 0.0 us)

commit v2 on v1

--- a/solution.py
+++ b/solution.py
@@ -46,6 +46,9 @@
     low_send,
     low_got,
     ss,
+    slot_of,
+    cosines,
+    sines,
     load_sem,
     w_sem,
     a_send_sem,
@@ -191,7 +194,7 @@
             device_id_type=MESH,
         )
 
-    ones = jnp.ones((8, feats), BF16)
+    ones = jnp.ones((8, 128), BF16)
     contract = (((1,), (1,)), ((), ()))
     for b in range(BLOCKS):
         h_copy[b].wait()
@@ -200,7 +203,9 @@
     def prepare(i, carry):
         sl = pl.ds(pl.multiple_of(i * step, step), step)
         h = hs[sl, :].astype(F32)
-        sq = h * h
+        sq = h[:, :128] * h[:, :128]
+        for c in range(1, feats // 128):
+            sq += h[:, c * 128 : (c + 1) * 128] * h[:, c * 128 : (c + 1) * 128]
         hi = sq.astype(BF16)
         lo = (sq - hi.astype(F32)).astype(BF16)
         total = lax.dot_general(ones, hi, contract, preferred_element_type=F32)
@@ -282,20 +287,35 @@
     for k in range(1, ranks):
         project(k)
 
-    def lowrank(slot, first):
+    lane = lax.broadcasted_iota(jnp.int32, (step, HD), 1)
+
+    def describe(i, carry):
+        sl = pl.ds(pl.multiple_of(i * step, step), step)
+        slot_of[sl, :] = jnp.broadcast_to(tok_ref[sl, 0:1], (step, HD))
+        angles = tok_ref[sl, 1:2].astype(F32) * freq_ref[...]
+        cosines[sl, :] = jnp.cos(angles)
+        sine = jnp.sin(angles)
+        sines[sl, :] = jnp.where(lane < HD // 2, -sine, sine)
+        return carry
+
+    lax.fori_loop(0, tokens // step, describe, 0)
+
+    def lowrank(source, first):
         def one(b, carry):
-            y = jnp.dot(hs[rows(b), :], got_a[slot], preferred_element_type=F32)
-            y = jnp.where(tok_ref[rows(b), 0:1] == slot, y, 0.0)
+            maps = jnp.concatenate([got_a[source * CAP], got_a[source * CAP + 1]], axis=1)
+            y = jnp.dot(hs[rows(b), :], maps, preferred_element_type=F32)
+            slot = slot_of[rows(b), :]
+            picked = jnp.where(slot == source * CAP, y[:, : 2 * rank], 0.0)
+            picked += jnp.where(slot == source * CAP + 1, y[:, 2 * rank :], 0.0)
             if first:
-                low[rows(b), :] = y
+                low[rows(b), :] = picked
             else:
-                low[rows(b), :] = low[rows(b), :] + y
+                low[rows(b), :] = low[rows(b), :] + picked
             return carry
 
         lax.fori_loop(0, BLOCKS, one, 0)
 
-    for s in range(CAP):
-        lowrank(me * CAP + s, s == 0)
+    lowrank(me, True)
 
     def forward(k):
         ju = last - k
@@ -336,7 +356,7 @@
         source = lax.rem(me + owners - k, owners)
         for s in range(CAP):
             a_move(k, source, s).wait_recv()
-            lowrank(source * CAP + s, False)
+        lowrank(source, False)
 
     def low_start(b, carry):
         mine = low[rows(b), :]
@@ -389,52 +409,54 @@
 
     slots = owners * CAP
 
-    def finish(b, carry):
+    def lift(b, carry):
         sl = rows(b)
-        total = part[t, sl, :]
-        lows = low[sl, :]
-
-        gains = jnp.sum(ss[:, :, sl], axis=0).T[:, 0:1]
-        gains = lax.rsqrt(gains * (1.0 / MODEL_WIDTH) + 1e-05)
-        part[t, sl, :] = total
 
         @pl.when(t > 0)
         def _():
-            up_copy(t, b).wait_recv()
-            part[t, sl, :] = part[t, sl, :] + got_up[t, sl, :].astype(F32)
             low[sl, :] = low[sl, :] + low_got[0, sl, :].astype(F32)
 
         @pl.when(t < last)
         def _():
-            dn_copy(t, b).wait_recv()
-            part[t, sl, :] = part[t, sl, :] + got_dn[t, sl, :].astype(F32)
             low[sl, :] = low[sl, :] + low_got[1, sl, :].astype(F32)
 
         lows = low[sl, :]
         hi = lows.astype(BF16).astype(F32)
         lo = lows - hi
-        mine = tok_ref[sl, 0:1]
-        picked_hi = jnp.concatenate(
-            [jnp.where(mine == s, hi, 0.0).astype(BF16) for s in range(slots)], axis=1
-        )
-        picked_lo = jnp.concatenate(
-            [jnp.where(mine == s, lo, 0.0).astype(BF16) for s in range(slots)], axis=1
-        )
+        slot = slot_of[sl, :]
         maps = got_b[...].reshape(slots * 2 * rank, 2 * cols)
         total = part[t, sl, :]
-        total += jnp.dot(picked_hi, maps, preferred_element_type=F32)
-        total += jnp.dot(picked_lo, maps, preferred_element_type=F32)
-        total = total * gains
+        for term in (hi, lo):
+            picked = jnp.concatenate(
+                [jnp.where(slot == s, term, 0.0).astype(BF16) for s in range(slots)], axis=1
+            )
+            total += jnp.dot(picked, maps, preferred_element_type=F32)
+        part[t, sl, :] = total
+        return carry
+
+    lax.fori_loop(0, BLOCKS, lift, 0)
+
+    def finish(b, carry):
+        sl = rows(b)
+        gains = jnp.sum(ss[:, :, sl], axis=0).T[:, 0:1]
+        gains = lax.rsqrt(gains * (1.0 / MODEL_WIDTH) + 1e-05)
+
+        @pl.when(t > 0)
+        def _():
+            up_copy(t, b).wait_recv()
+            part[t, sl, :] = part[t, sl, :] + got_up[t, sl, :].astype(F32)
+
+        @pl.when(t < last)
+        def _():
+            dn_copy(t, b).wait_recv()
+            part[t, sl, :] = part[t, sl, :] + got_dn[t, sl, :].astype(F32)
+
+        total = part[t, sl, :] * gains
         value_ref[sl, :] = total[:, cols:].astype(BF16)
-        angles = tok_ref[sl, 1:2].astype(F32) * freq_ref[...]
-        cosine = jnp.cos(angles)
-        sine = jnp.sin(angles)
-        lane = lax.broadcasted_iota(jnp.int32, sine.shape, 1)
-        sine = jnp.where(lane < HD // 2, -sine, sine)
         for head in range(cols // HD):
             x = total[:, head * HD : (head + 1) * HD]
             key_ref[sl, pl.ds(head * HD, HD)] = (
-                x * cosine + pltpu.roll(x, HD // 2, 1) * sine
+                x * cosines[sl, :] + pltpu.roll(x, HD // 2, 1) * sines[sl, :]
             ).astype(BF16)
         return carry
 
@@ -556,6 +578,9 @@
             pltpu.VMEM((2, tokens, 2 * rank), BF16),
             pltpu.VMEM((2, tokens, 2 * rank), BF16),
             pltpu.VMEM((ranks, 8, tokens), F32),
+            pltpu.VMEM((tokens, HD), jnp.int32),
+            pltpu.VMEM((tokens, HD), F32),
+            pltpu.VMEM((tokens, HD), F32),
             dma((2 + BLOCKS,)),
             dma((ranks,)),
             dma((owners, CAP)),

time: 163 us -> 162 us (level)
  no operation moved by 1% of the time
where the time goes in v2:
time: 162 us
  Pallas kernels  131 us (81%)
  local copies, waits for them, and re-layouts  16.4 us (10%)
  blocking collectives  6.38 us (4%)
  other arithmetic  6.2 us (4%)
    pallas_call x1, Pallas kernels, body(): pl.pallas_call(functools.partial(kernel, owners, ranks), out_shape=(jax.S...  131 us
    unnamed x6, local copies, waits for them, and re-layouts  15.1 us
    unnamed x1, blocking collectives  6.38 us

profile of v2, /device:TPU:0, one launch (start us, length us, event | category | flops | bytes accessed | tf_op | source)
XLA Modules:
  0.0 161.7 jit_solution(13422324798934774887)
XLA Ops:
  0.6 1.2 dynamic-slice
  2.5 0.9 select_reduce_fusion.4
  3.4 0.8 select_reduce_fusion.5
  4.2 0.7 fusion.9
  4.8 0.2 select_reduce_fusion.3
  5.0 0.9 dynamic-update-slice
  5.9 6.4 %all-reduce = s32[64]{0:T(128)S(1)} all-reduce(s32[64]{0:T(128)S(1)} %dynamic-update-slice), channel_id=1, replica_groups=mesh['groups'=2,'adapters'=4,'tensor'=4] {'adapters'}, use_global_device_ids=true, to_apply=%add | all-reduce | flops 64 | bytes 512
  12.3 0.6 fusion.8.freq_ref
  12.9 0.1 eq.51
  13.0 0.9 select_reduce_fusion.2
  13.8 0.2 select_reduce_fusion.7
  14.0 0.1 copy.23
  14.1 0.1 copy.22
  14.2 0.7 pad_add_fusion.1.rows_ref
  14.9 0.1 select_reduce_fusion.1
  15.0 1.3 broadcast_in_dim.79
  16.3 1.0 copy.25.tok_ref
  17.3 9.3 %copy.27 = bf16[2048,2,1024]{2,0,1:T(8,128)(2,1)} copy(bf16[2048,2,1024]{2,1,0:T(2,128)(2,1)} %param.10) | data formatting | bytes 16777216 | tf_op args[2]
  26.6 131.4 %shard_map.95 = (bf16[1024,256]{1,0:T(8,128)(2,1)}, bf16[1024,256]{1,0:T(8,128)(2,1)}) custom-call(s32[4,2]{1,0:T(4,128)} %pad_add_fusion.1.rows_ref, s32[1024,2]{1,0:T(8,128)} %copy.25.tok_ref, f32[1,128]{1,0:T(1,128)} %fusion.8.freq_ref, f32[1,2048]{1,0:T(1,128)} %bitcast.19, bf16[1024,2048]{1,0:T(8,128)(2,1)} %h_hbm.1, bf16[2,2048,1024]{2,1,0:T(8,128)(2,1)} %bitcast.16, ...), custom_call_target="tpu_custom_call" | custom-call | flops 12884901888 | bytes 20971520 | tf_op jit(solution)/shard_map/pallas_call | solution.py:556
  157.9 1.9 %copy.31 = bf16[1024,256]{1,0:T(8,128)(2,1)} copy(bf16[1024,256]{1,0:T(8,128)(2,1)} %get-tuple-element.8) | data formatting | bytes 1048576
  159.8 1.9 %copy.32 = bf16[1024,256]{1,0:T(8,128)(2,1)} copy(bf16[1024,256]{1,0:T(8,128)(2,1)} %get-tuple-element.9) | data formatting | bytes 1048576
  (4 shorter events, 0.0 us)
